TPU v7x, 32 devices: a whole 2x2x4 slice. The times are simulated.
32 devices in a mesh: tm: 8 (over z, y), rep: 4 (over x, core).
Axes of the slice: x: 2, y: 2, z: 4, core: 2. Of those that a mesh axis runs over, the one named last changes fastest.
Arguments:
- separator_inverse: bfloat16 [32, 384, 384], P(('rep', 'tm')), parts along dimension 0, may hold values from -1 to 3, as said below
- separator_lower: bfloat16 [32, 384, 384], P(('rep', 'tm')), parts along dimension 0, may hold values from -0.15625 to 0.15625
- separator_upper: bfloat16 [32, 384, 384], P(('rep', 'tm')), parts along dimension 0, may hold values from -0.15625 to 0.15625
- top_diagonal: bfloat16 [32, 384, 384], P(('rep', 'tm')), parts along dimension 0, may hold values from -1 to 3, as said below
- top_coupling: bfloat16 [32, 384, 384], P(('rep', 'tm')), parts along dimension 0, may hold values from -0.3125 to 0.3125
- interior_inverse: bfloat16 [32, 384, 384], P(('rep', 'tm')), parts along dimension 0, may hold values from -1 to 3, as said below
- interior_lower: bfloat16 [32, 384, 384], P(('rep', 'tm')), parts along dimension 0, may hold values from -0.15625 to 0.15625
- interior_upper: bfloat16 [32, 384, 384], P(('rep', 'tm')), parts along dimension 0, may hold values from -0.15625 to 0.15625
Outputs:
- inverse_diagonal: bfloat16 [64, 384, 384], P(('rep', 'tm')), parts along dimension 0
- inverse_below: bfloat16 [64, 384, 384], P(('rep', 'tm')), parts along dimension 0
There are 4 independent parts, one for each index of `rep`. A program takes and returns all parts, laid end to end along the dimension named above; each array names one. Nothing has to cross between parts.
Inputs may be any that keep to these rules, and one draw needn't show every extreme that they name: `separator_inverse`: every block is symmetric. `top_diagonal`: every block is symmetric. `interior_inverse`: every block is symmetric.
All inputs are finite; a program needn't handle non-finite values.
Results may differ from a plain program's by a relative error of at most 0.006.
Values may be sent and summed in bfloat16 or wider, within the bound.
A program may use at most 64 MiB of HBM per device.

v0:
```python
import jax
import jax.numpy as jnp
from jax import lax
from jax.sharding import PartitionSpec as P


def shifted(value, axis, steps):
    count = lax.axis_size(axis)
    pairs = [(source, (source + steps) % count) for source in range(count)]
    return lax.ppermute(value, axis, pairs)


def product(left_op, right_op):
    return jnp.dot(left_op, right_op, preferred_element_type=jnp.float32)


def product_transposed(left_op, right_op):
    return lax.dot_general(
        left_op, right_op, (((1,), (1,)), ((), ())), preferred_element_type=jnp.float32
    )


def descend(inverse, lower_mult, upper_mult, lower_diagonal, coupling, upper_diagonal):
    toward_lower = (product(lower_mult, lower_diagonal) + product(upper_mult, coupling)).astype(
        jnp.bfloat16
    )
    toward_upper = (
        product_transposed(lower_mult, coupling) + product(upper_mult, upper_diagonal)
    ).astype(jnp.bfloat16)
    diagonal_new = (
        inverse.astype(jnp.float32)
        + product_transposed(toward_lower, lower_mult)
        + product_transposed(toward_upper, upper_mult)
    ).astype(jnp.bfloat16)
    return (toward_lower, toward_upper, diagonal_new)


def on_device(
    separator_inverse,
    separator_lower,
    separator_upper,
    top_diagonal,
    top_coupling,
    interior_inverse,
    interior_lower,
    interior_upper,
):
    devices = lax.axis_size("tm")
    levels_total = min(4, devices // 4)
    spacing = 2**levels_total
    position = (lax.axis_index("tm") + spacing // 2) % devices
    blank = jnp.zeros(separator_inverse.shape[1:], jnp.bfloat16)
    topmost = position % spacing == 0
    sigma_diagonal = jnp.where(topmost, top_diagonal[0], blank)
    sigma_upper = jnp.where(topmost, top_coupling[0], blank)
    sigma_lower = blank
    for height in range(levels_total, 0, -1):
        offset = 2 ** (height - 1)
        stride = 2 * offset
        lower_diagonal, lower_coupling = shifted((sigma_diagonal, sigma_upper), "tm", offset)
        upper_diagonal, upper_coupling = shifted((sigma_diagonal, sigma_lower), "tm", -offset)
        lower_holds = jnp.logical_or(height == levels_total, position // stride % 2 == 1)
        coupling = jnp.where(lower_holds, lower_coupling.T, upper_coupling)
        removed = position % stride == offset
        toward_lower, toward_upper, diagonal_new = descend(
            separator_inverse[0],
            separator_lower[0],
            separator_upper[0],
            lower_diagonal,
            coupling,
            upper_diagonal,
        )
        sigma_lower = jnp.where(removed, toward_lower, sigma_lower)
        sigma_upper = jnp.where(removed, toward_upper, sigma_upper)
        sigma_diagonal = jnp.where(removed, diagonal_new, sigma_diagonal)
    next_diagonal, next_lower = shifted((sigma_diagonal, sigma_lower), "tm", -1)
    coupling = jnp.where(position % 2 == 1, sigma_upper.T, next_lower)
    below_own, below_next, interior_diagonal = descend(
        interior_inverse[0],
        interior_lower[0],
        interior_upper[0],
        sigma_diagonal,
        coupling,
        next_diagonal,
    )
    return (jnp.stack([sigma_diagonal, interior_diagonal]), jnp.stack([below_own, below_next.T]))


def solution(mesh):
    in_specs = (
        P(("rep", "tm"), None, None),
        P(("rep", "tm"), None, None),
        P(("rep", "tm"), None, None),
        P(("rep", "tm"), None, None),
        P(("rep", "tm"), None, None),
        P(("rep", "tm"), None, None),
        P(("rep", "tm"), None, None),
        P(("rep", "tm"), None, None),
    )
    out_specs = (P(("rep", "tm"), None, None), P(("rep", "tm"), None, None))
    return jax.shard_map(
        on_device, mesh=mesh, in_specs=in_specs, out_specs=out_specs, check_vma=False
    )
```

profile of v0, /device:TPU:0, one launch (start us, length us, event | category | flops | bytes accessed | tf_op | source)
XLA Modules:
  0.0 72.6 jit_solution(469371538781455236)
XLA Ops:
  0.6 0.0 copy-start
  0.7 0.0 copy-start.5
  0.7 0.0 copy-start.1
  0.8 4.1 %collective-permute-start.1 = (bf16[384,384]{1,0:T(8,128)(2,1)S(1)}, bf16[384,384]{1,0:T(8,128)(2,1)S(1)}, u32[]{:S(2)}, u32[]{:S(2)}) collective-permute-start(bf16[384,384]{1,0:T(8,128)(2,1)S(1)} %select_bitcast_fusion.1), channel_id=1, source_target_pairs={{0,8},{4,12},{8,16},{12,20},{16,24},{20,28},{24,0},{28,4},{1,9},{5... | collective-permute-start | bytes 884744 | tf_op jit(solution)/shard_map/ppermute | solution.py:10
  4.8 0.0 copy-done.5
  4.9 0.6 collective-permute-start
  5.5 3.3 %collective-permute-start.2 = (bf16[384,384]{1,0:T(8,128)(2,1)S(1)}, bf16[384,384]{1,0:T(8,128)(2,1)S(1)}, u32[]{:S(2)}, u32[]{:S(2)}) collective-permute-start(bf16[384,384]{1,0:T(8,128)(2,1)S(1)} %select_bitcast_fusion.2), channel_id=1, source_target_pairs={{0,24},{4,28},{8,0},{12,4},{16,8},{20,12},{24,16},{28,20},{1,25},{... | collective-permute-start | bytes 884744 | tf_op jit(solution)/shard_map/ppermute | solution.py:10
  8.7 6.1 %collective-permute-done.1 = bf16[384,384]{1,0:T(8,128)(2,1)S(1)} collective-permute-done((bf16[384,384]{1,0:T(8,128)(2,1)S(1)}, bf16[384,384]{1,0:T(8,128)(2,1)S(1)}, u32[]{:S(2)}, u32[]{:S(2)}) %collective-permute-start.1) | collective-permute-done | bytes 294944 | tf_op jit(solution)/shard_map/ppermute | solution.py:10
  14.8 0.0 copy-done.1
  14.8 0.3 fusion.28
  15.2 5.9 %collective-permute-done = bf16[384,384]{1,0:T(8,128)(2,1)S(1)} collective-permute-done((bf16[384,384]{1,0:T(8,128)(2,1)S(1)}, bf16[384,384]{1,0:T(8,128)(2,1)S(1)}, u32[]{:S(2)}, u32[]{:S(2)}) %collective-permute-start) | collective-permute-done | bytes 294944 | tf_op jit(solution)/shard_map/ppermute | solution.py:10
  21.1 0.0 copy-done
  21.1 0.4 fusion
  21.5 0.0 copy-start.4
  21.5 0.9 %copy-done.4 = bf16[1,384,384]{2,1,0:T(8,128)(2,1)S(1)} copy-done((bf16[1,384,384]{2,1,0:T(8,128)(2,1)S(1)}, bf16[1,384,384]{2,1,0:T(8,128)(2,1)}, u32[]{:S(2)}) %copy-start.4) | copy-done | bytes 294936
  22.4 0.4 convolution_add_fusion.10
  22.9 3.7 %collective-permute-done.2 = bf16[384,384]{1,0:T(8,128)(2,1)S(1)} collective-permute-done((bf16[384,384]{1,0:T(8,128)(2,1)S(1)}, bf16[384,384]{1,0:T(8,128)(2,1)S(1)}, u32[]{:S(2)}, u32[]{:S(2)}) %collective-permute-start.2) | collective-permute-done | bytes 294944 | tf_op jit(solution)/shard_map/ppermute | solution.py:10
  26.5 0.3 fusion.21
  26.8 0.4 bitcast_select_fusion.4
  27.2 0.6 collective-permute-start.4
  27.8 4.2 %collective-permute-start.5 = (bf16[384,384]{0,1:T(8,128)(2,1)S(1)}, bf16[384,384]{0,1:T(8,128)(2,1)S(1)}, u32[]{:S(2)}, u32[]{:S(2)}) collective-permute-start(bf16[384,384]{0,1:T(8,128)(2,1)S(1)} %select_bitcast_fusion), channel_id=1, source_target_pairs={{0,28},{4,0},{8,4},{12,8},{16,12},{20,16},{24,20},{28,24},{1,29},{... | collective-permute-start | bytes 884744 | tf_op jit(solution)/shard_map/ppermute | solution.py:10
  32.0 0.4 fusion.11
  32.4 0.1 collective-permute-start.3
  32.5 4.7 %collective-permute-start.6 = (bf16[384,384]{1,0:T(8,128)(2,1)S(1)}, bf16[384,384]{1,0:T(8,128)(2,1)S(1)}, u32[]{:S(2)}, u32[]{:S(2)}) collective-permute-start(bf16[384,384]{1,0:T(8,128)(2,1)S(1)} %fusion.11), channel_id=1, source_target_pairs={{0,28},{4,0},{8,4},{12,8},{16,12},{20,16},{24,20},{28,24},{1,29},{... | collective-permute-start | bytes 884744 | tf_op jit(solution)/shard_map/ppermute | solution.py:10
  37.1 10.7 %collective-permute-done.4 = bf16[384,384]{1,0:T(8,128)(2,1)S(1)} collective-permute-done((bf16[384,384]{1,0:T(8,128)(2,1)S(1)}, bf16[384,384]{1,0:T(8,128)(2,1)S(1)}, u32[]{:S(2)}, u32[]{:S(2)}) %collective-permute-start.4) | collective-permute-done | bytes 294944 | tf_op jit(solution)/shard_map/ppermute | solution.py:10
  47.8 2.5 %collective-permute-done.5 = bf16[384,384]{0,1:T(8,128)(2,1)S(1)} collective-permute-done((bf16[384,384]{0,1:T(8,128)(2,1)S(1)}, bf16[384,384]{0,1:T(8,128)(2,1)S(1)}, u32[]{:S(2)}, u32[]{:S(2)}) %collective-permute-start.5) | collective-permute-done | bytes 294944 | tf_op jit(solution)/shard_map/ppermute | solution.py:10
  50.3 0.3 fusion.23
  50.7 2.5 %collective-permute-done.3 = bf16[384,384]{1,0:T(8,128)(2,1)S(1)} collective-permute-done((bf16[384,384]{1,0:T(8,128)(2,1)S(1)}, bf16[384,384]{1,0:T(8,128)(2,1)S(1)}, u32[]{:S(2)}, u32[]{:S(2)}) %collective-permute-start.3) | collective-permute-done | bytes 294944 | tf_op jit(solution)/shard_map/ppermute | solution.py:10
  53.2 0.4 bitcast_select_fusion
  53.6 3.3 %collective-permute-start.7 = (bf16[384,384]{0,1:T(8,128)(2,1)S(1)}, bf16[384,384]{0,1:T(8,128)(2,1)S(1)}, u32[]{:S(2)}, u32[]{:S(2)}) collective-permute-start(bf16[384,384]{0,1:T(8,128)(2,1)S(1)} %get-tuple-element.6), channel_id=1, source_target_pairs={{0,28},{4,0},{8,4},{12,8},{16,12},{20,16},{24,20},{28,24},{1,29},{... | collective-permute-start | bytes 884744 | tf_op jit(solution)/shard_map/ppermute | solution.py:10
  56.9 0.4 convolution_add_fusion.7
  57.3 0.0 collective-permute-done.6
  57.3 0.3 fusion.26
  57.6 0.3 fusion.7
  58.0 0.0 copy-start.2
  58.0 0.4 fusion.10
  58.4 0.1 collective-permute-start.8
  58.4 0.5 copy-done.2
  59.0 0.4 fusion.18
  59.4 0.0 copy-start.3
  59.4 4.7 %collective-permute-done.7 = bf16[384,384]{0,1:T(8,128)(2,1)S(1)} collective-permute-done((bf16[384,384]{0,1:T(8,128)(2,1)S(1)}, bf16[384,384]{0,1:T(8,128)(2,1)S(1)}, u32[]{:S(2)}, u32[]{:S(2)}) %collective-permute-start.7) | collective-permute-done | bytes 294944 | tf_op jit(solution)/shard_map/ppermute | solution.py:10
  64.0 0.1 bitcast_select_fusion.1
  64.1 4.7 %collective-permute-done.8 = bf16[384,384]{1,0:T(8,128)(2,1)S(1)} collective-permute-done((bf16[384,384]{1,0:T(8,128)(2,1)S(1)}, bf16[384,384]{1,0:T(8,128)(2,1)S(1)}, u32[]{:S(2)}, u32[]{:S(2)}) %collective-permute-start.8) | collective-permute-done | bytes 294944 | tf_op jit(solution)/shard_map/ppermute | solution.py:10
  68.8 0.0 copy-done.3
  68.8 0.3 fusion.13
  69.1 0.3 fusion.8
  69.4 0.4 fusion.4
  69.8 0.1 pad_maximum_fusion.1
  69.9 0.0 copy-start.6
  69.9 1.1 %copy.18 = bf16[2,384,384]{2,1,0:T(8,128)(2,1)} copy(bf16[2,384,384]{1,2,0:T(8,128)(2,1)S(1)} %pad_maximum_fusion.1) | data formatting | bytes 1179648
  71.0 0.0 copy-done.6
  71.0 0.4 convolution_add_fusion.4
  71.4 0.3 fusion.9
  71.7 0.9 %pad_maximum_fusion = bf16[2,384,384]{2,1,0:T(8,128)(2,1)} fusion(bf16[1,384,384]{2,1,0:T(8,128)(2,1)S(1)} %fusion.9, bf16[1,384,384]{2,1,0:T(8,128)(2,1)S(1)} %bitcast.94), kind=kLoop, calls=%fused_computation.24 | loop fusion | flops 294912 | bytes 1179648 | tf_op jit(solution)/shard_map/stack | solution.py:86
  (3 shorter events, 0.1 us)
Async XLA Ops:
  0.6 20.4 %copy-start = (bf16[1,384,384]{2,1,0:T(8,128)(2,1)S(1)}, bf16[1,384,384]{2,1,0:T(8,128)(2,1)}, u32[]{:S(2)}) copy-start(bf16[1,384,384]{2,1,0:T(8,128)(2,1)} %param.9) | copy-start | bytes 884740
  0.7 4.2 %copy-start.5 = (bf16[1,384,384]{2,1,0:T(8,128)(2,1)S(1)}, bf16[1,384,384]{2,1,0:T(8,128)(2,1)}, u32[]{:S(2)}) copy-start(bf16[1,384,384]{2,1,0:T(8,128)(2,1)} %param.11) | copy-start | bytes 884740
  0.7 14.1 %copy-start.1 = (bf16[1,384,384]{2,1,0:T(8,128)(2,1)S(1)}, bf16[1,384,384]{2,1,0:T(8,128)(2,1)}, u32[]{:S(2)}) copy-start(bf16[1,384,384]{2,1,0:T(8,128)(2,1)} %param.10) | copy-start | bytes 884740
  0.8 14.1 %collective-permute-start.1 = (bf16[384,384]{1,0:T(8,128)(2,1)S(1)}, bf16[384,384]{1,0:T(8,128)(2,1)S(1)}, u32[]{:S(2)}, u32[]{:S(2)}) collective-permute-start(bf16[384,384]{1,0:T(8,128)(2,1)S(1)} %select_bitcast_fusion.1), channel_id=1, source_target_pairs={{0,8},{4,12},{8,16},{12,20},{16,24},{20,28},{24,0},{28,4},{1,9},{5... | collective-permute-start | bytes 884744 | tf_op jit(solution)/shard_map/ppermute | solution.py:10
  4.9 16.2 %collective-permute-start = (bf16[384,384]{1,0:T(8,128)(2,1)S(1)}, bf16[384,384]{1,0:T(8,128)(2,1)S(1)}, u32[]{:S(2)}, u32[]{:S(2)}) collective-permute-start(bf16[384,384]{1,0:T(8,128)(2,1)S(1)} %select_bitcast_fusion.2), channel_id=1, source_target_pairs={{0,8},{4,12},{8,16},{12,20},{16,24},{20,28},{24,0},{28,4},{1,9},{5... | collective-permute-start | bytes 884744 | tf_op jit(solution)/shard_map/ppermute | solution.py:10
  5.5 21.0 %collective-permute-start.2 = (bf16[384,384]{1,0:T(8,128)(2,1)S(1)}, bf16[384,384]{1,0:T(8,128)(2,1)S(1)}, u32[]{:S(2)}, u32[]{:S(2)}) collective-permute-start(bf16[384,384]{1,0:T(8,128)(2,1)S(1)} %select_bitcast_fusion.2), channel_id=1, source_target_pairs={{0,24},{4,28},{8,0},{12,4},{16,8},{20,12},{24,16},{28,20},{1,25},{... | collective-permute-start | bytes 884744 | tf_op jit(solution)/shard_map/ppermute | solution.py:10
  21.5 1.0 %copy-start.4 = (bf16[1,384,384]{2,1,0:T(8,128)(2,1)S(1)}, bf16[1,384,384]{2,1,0:T(8,128)(2,1)}, u32[]{:S(2)}) copy-start(bf16[1,384,384]{2,1,0:T(8,128)(2,1)} %param.8) | copy-start | bytes 884740
  27.2 20.6 %collective-permute-start.4 = (bf16[384,384]{1,0:T(8,128)(2,1)S(1)}, bf16[384,384]{1,0:T(8,128)(2,1)S(1)}, u32[]{:S(2)}, u32[]{:S(2)}) collective-permute-start(bf16[384,384]{1,0:T(8,128)(2,1)S(1)} %get-tuple-element.4), channel_id=1, source_target_pairs={{0,4},{4,8},{8,12},{12,16},{16,20},{20,24},{24,28},{28,0},{1,5},{5... | collective-permute-start | bytes 884744 | tf_op jit(solution)/shard_map/ppermute | solution.py:10
  27.8 22.6 %collective-permute-start.5 = (bf16[384,384]{0,1:T(8,128)(2,1)S(1)}, bf16[384,384]{0,1:T(8,128)(2,1)S(1)}, u32[]{:S(2)}, u32[]{:S(2)}) collective-permute-start(bf16[384,384]{0,1:T(8,128)(2,1)S(1)} %select_bitcast_fusion), channel_id=1, source_target_pairs={{0,28},{4,0},{8,4},{12,8},{16,12},{20,16},{24,20},{28,24},{1,29},{... | collective-permute-start | bytes 884744 | tf_op jit(solution)/shard_map/ppermute | solution.py:10
  32.4 20.8 %collective-permute-start.3 = (bf16[384,384]{1,0:T(8,128)(2,1)S(1)}, bf16[384,384]{1,0:T(8,128)(2,1)S(1)}, u32[]{:S(2)}, u32[]{:S(2)}) collective-permute-start(bf16[384,384]{1,0:T(8,128)(2,1)S(1)} %fusion.11), channel_id=1, source_target_pairs={{0,4},{4,8},{8,12},{12,16},{16,20},{20,24},{24,28},{28,0},{1,5},{5... | collective-permute-start | bytes 884744 | tf_op jit(solution)/shard_map/ppermute | solution.py:10
  32.5 24.8 %collective-permute-start.6 = (bf16[384,384]{1,0:T(8,128)(2,1)S(1)}, bf16[384,384]{1,0:T(8,128)(2,1)S(1)}, u32[]{:S(2)}, u32[]{:S(2)}) collective-permute-start(bf16[384,384]{1,0:T(8,128)(2,1)S(1)} %fusion.11), channel_id=1, source_target_pairs={{0,28},{4,0},{8,4},{12,8},{16,12},{20,16},{24,20},{28,24},{1,29},{... | collective-permute-start | bytes 884744 | tf_op jit(solution)/shard_map/ppermute | solution.py:10
  53.6 10.5 %collective-permute-start.7 = (bf16[384,384]{0,1:T(8,128)(2,1)S(1)}, bf16[384,384]{0,1:T(8,128)(2,1)S(1)}, u32[]{:S(2)}, u32[]{:S(2)}) collective-permute-start(bf16[384,384]{0,1:T(8,128)(2,1)S(1)} %get-tuple-element.6), channel_id=1, source_target_pairs={{0,28},{4,0},{8,4},{12,8},{16,12},{20,16},{24,20},{28,24},{1,29},{... | collective-permute-start | bytes 884744 | tf_op jit(solution)/shard_map/ppermute | solution.py:10
  58.0 1.0 %copy-start.2 = (bf16[1,384,384]{2,1,0:T(8,128)(2,1)S(1)}, bf16[1,384,384]{2,1,0:T(8,128)(2,1)}, u32[]{:S(2)}) copy-start(bf16[1,384,384]{2,1,0:T(8,128)(2,1)} %param.14) | copy-start | bytes 884740
  58.4 10.4 %collective-permute-start.8 = (bf16[384,384]{1,0:T(8,128)(2,1)S(1)}, bf16[384,384]{1,0:T(8,128)(2,1)S(1)}, u32[]{:S(2)}, u32[]{:S(2)}) collective-permute-start(bf16[384,384]{1,0:T(8,128)(2,1)S(1)} %fusion.10), channel_id=1, source_target_pairs={{0,28},{4,0},{8,4},{12,8},{16,12},{20,16},{24,20},{28,24},{1,29},{... | collective-permute-start | bytes 884744 | tf_op jit(solution)/shard_map/ppermute | solution.py:10
  59.4 9.4 %copy-start.3 = (bf16[1,384,384]{2,1,0:T(8,128)(2,1)S(1)}, bf16[1,384,384]{2,1,0:T(8,128)(2,1)}, u32[]{:S(2)}) copy-start(bf16[1,384,384]{2,1,0:T(8,128)(2,1)} %param.15) | copy-start | bytes 884740
  69.9 1.1 %copy-start.6 = (bf16[1,384,384]{2,1,0:T(8,128)(2,1)S(1)}, bf16[1,384,384]{2,1,0:T(8,128)(2,1)}, u32[]{:S(2)}) copy-start(bf16[1,384,384]{2,1,0:T(8,128)(2,1)} %param.13) | copy-start | bytes 884740
where the time goes:
time: 72.8 us; the launch traced here: 72.6 us
  waiting for transfers between devices  40.6 us (56%)
  starting transfers between devices  20.8 us (29%)
  matrix products  6.53 us (9%)
  local copies, waits for them, and re-layouts  2.53 us (3%)
  other arithmetic  1.11 us (2%)
  between operations  0.96 us (1%)
    ppermute x9, waiting for transfers between devices, shifted(): return lax.ppermute(value, axis, pairs)  40.6 us
    ppermute x9, starting transfers between devices, shifted(): return lax.ppermute(value, axis, pairs)  20.8 us
    dot_general x9, matrix products, product_transposed(): lax.dot_general(left_op, right_op, (((1,), (1,)), ((), ())), preferred_el...  3.3 us
    dot_general x9, matrix products, product(): return jnp.dot(left_op, right_op, preferred_element_type=jnp.float32)  3.23 us
    unnamed x15, local copies, waits for them, and re-layouts  2.53 us
  transfers between devices with their start and end apart: 9, of which 8 were waited for; matrix products, arithmetic and copies ran while one was open for 6% of the time, Pallas kernels for 0%

commit v1 on v0

v1 whole, which is shorter than its diff:
```python
import functools

import jax
import jax.numpy as jnp
from jax import lax
from jax.experimental import pallas as pl
from jax.experimental.pallas import tpu as pltpu
from jax.sharding import PartitionSpec as P

MESH = pl.DeviceIdType.MESH
TILE = 128


def product(left_op, right_op):
    return jnp.dot(left_op, right_op, preferred_element_type=jnp.float32)


def product_transposed(left_op, right_op):
    return lax.dot_general(
        left_op, right_op, (((1,), (1,)), ((), ())), preferred_element_type=jnp.float32
    )


def strips(size):
    tile = TILE if size % TILE == 0 else size
    return [(at, tile) for at in range(0, size, tile)]


def strip(ref, at, rows):
    size = ref.shape[-1]
    return ref.at[pl.ds(at, rows), pl.ds(at, size - at)]


def mirror(ref):
    for at, rows in strips(ref.shape[-1]):
        for other, others in strips(ref.shape[-1]):
            if other > at:
                ref[pl.ds(other, others), pl.ds(at, rows)] = ref[
                    pl.ds(at, rows), pl.ds(other, others)
                ].T


class Mail:
    def __init__(self, dst, send_sem, send_at, recv_sem, recv_at, symmetric):
        self.dst, self.symmetric = dst, symmetric
        self.send_sem, self.send_at = send_sem, send_at
        self.recv_sem, self.recv_at = recv_sem, recv_at
        self.pieces = strips(dst.shape[-1]) if symmetric else [None]

    def copy(self, src, to, piece):
        dst = self.dst
        if self.symmetric:
            src, dst = strip(src, *self.pieces[piece]), strip(dst, *self.pieces[piece])
        return pltpu.make_async_remote_copy(
            src_ref=src,
            dst_ref=dst,
            send_sem=self.send_sem.at[self.send_at + piece],
            recv_sem=self.recv_sem.at[self.recv_at + piece],
            device_id={"tm": to},
            device_id_type=MESH,
        )

    def start(self, src, to):
        for piece in range(len(self.pieces)):
            self.copy(src, to, piece).start()

    def wait_send(self, src, to):
        for piece in range(len(self.pieces)):
            self.copy(src, to, piece).wait_send()

    def wait_recv(self, to):
        for piece in range(len(self.pieces)):
            self.copy(self.dst, to, piece).wait_recv()

    def relay(self, incoming, to):
        for piece in range(len(self.pieces)):
            incoming.copy(incoming.dst, to, piece).wait_recv()
            self.copy(incoming.dst, to, piece).start()


def semaphore_counts(levels, pieces):
    per_level = 2 * pieces + 2
    sends = (levels - 1) * per_level + (1 + pieces) + (1 + 2 * pieces) + (2 + pieces)
    receives = (1 + 2 * pieces) + (3 + 3 * pieces)
    return sends, receives


def kernel(
    devices,
    levels,
    sep_inv,
    sep_lower,
    sep_upper,
    top_diag,
    top_coup,
    int_inv,
    int_lower,
    int_upper,
    out_diag,
    out_below,
    inv,
    low,
    upp,
    diag,
    up,
    down,
    diag_a,
    diag_b,
    coup,
    inv1,
    low1,
    upp1,
    diag_a1,
    diag_b1,
    coup1,
    up1,
    down1,
    diag1,
    iinv,
    ilow,
    iupp,
    idiag,
    below,
    below_t,
    send_sem,
    recv_sem,
    load_sem,
    store_sem,
):
    size = sep_inv.shape[-1]
    pieces = len(strips(size))
    spacing = 2**levels
    me = lax.axis_index("tm")
    position = lax.rem(me + spacing // 2, devices)
    odd = lax.rem(position, 2) == 1
    even = lax.rem(position, 2) == 0
    top = lax.rem(position, spacing) == 0

    def near(steps):
        return lax.rem(me + steps + devices, devices)

    def load(src, dst, at):
        return pltpu.make_async_copy(src.at[0], dst, load_sem.at[at])

    def store(src, dst, at):
        return pltpu.make_async_copy(src, dst, store_sem.at[at])

    counts = {"send": 0, "recv": 0}

    def take(kind, number):
        counts[kind] += number
        return counts[kind] - number

    def receives(symmetric):
        return take("recv", pieces if symmetric else 1)

    def mail(dst, recv_at, symmetric):
        send_at = take("send", pieces if symmetric else 1)
        return Mail(dst, send_sem, send_at, recv_sem, recv_at, symmetric)

    at_a, at_b, at_c = receives(True), receives(True), receives(False)
    at_a1, at_b1, at_c1 = receives(True), receives(True), receives(False)
    at_inv1, at_low1, at_upp1 = receives(True), receives(False), receives(False)
    level_mail = {}
    for height in range(levels, 1, -1):
        level_mail[height] = dict(
            a=mail(diag_a, at_a, True),
            b=mail(diag_b, at_b, True),
            c_up=mail(coup, at_c, False),
            c_down=mail(coup, at_c, False),
        )
    feed_c, feed_b = mail(coup1, at_c1, False), mail(diag_b1, at_b1, True)
    odd_a, odd_b, odd_c = mail(diag_a1, at_a1, True), mail(diag_b1, at_b1, True), mail(coup1, at_c1, False)
    back_inv, back_low, back_upp = (
        mail(inv1, at_inv1, True),
        mail(low1, at_low1, False),
        mail(upp1, at_upp1, False),
    )

    @pl.when(even)
    def _():
        load(sep_lower, low, 0).start()
        load(sep_upper, upp, 1).start()
        load(sep_inv, inv, 2).start()

    @pl.when(odd)
    def _():
        load(sep_lower, low1, 0).start()
        load(sep_upper, upp1, 1).start()
        load(sep_inv, inv1, 2).start()

    @pl.when(top)
    def _():
        load(top_diag, diag, 3).start()

    load(int_lower, ilow, 5).start()
    load(int_upper, iupp, 6).start()
    load(int_inv, iinv, 7).start()

    barrier = pltpu.get_barrier_semaphore()
    reach = [sign * 2**power for power in range(levels) for sign in (1, -1)]
    for steps in reach:
        pl.semaphore_signal(barrier, inc=1, device_id={"tm": near(steps)}, device_id_type=MESH)
    pl.semaphore_wait(barrier, len(reach))

    def holds(height):
        return lax.rem(position, 2**height) == 0

    def coupled(height):
        return lax.rem(position // 2**height, 2) == 1

    def sends(height, act):
        offset = 2 ** (height - 1)
        mails = level_mail[height]
        if height == levels:
            diag_src, up_src = top_diag.at[0], top_coup.at[0]
        else:
            diag_src, up_src = diag, up

        def act_up():
            act(mails["c_up"], up_src, near(offset))

        def act_down():
            act(mails["c_down"], down, near(-offset))

        if height == levels:
            act_up()
        else:
            pl.when(coupled(height))(act_up)
            pl.when(coupled(height))(act_down)
        act(mails["b"], diag_src, near(-offset))
        act(mails["a"], diag_src, near(offset))

    def start(message, src, to):
        message.start(src, to)

    def finish(message, src, to):
        message.wait_send(src, to)

    pl.when(holds(levels))(lambda: sends(levels, start))

    @pl.when(odd)
    def _():
        back_low.start(sep_lower.at[0], near(-1))
        back_upp.start(sep_upper.at[0], near(-1))
        back_inv.start(sep_inv.at[0], near(-1))

    @pl.when(even)
    def _():
        load(sep_lower, low, 0).wait()
        load(sep_upper, upp, 1).wait()
        load(sep_inv, inv, 2).wait()

    @pl.when(top)
    def _():
        load(top_diag, diag, 3).wait()

    parent = lax.rem(position, 4) == 2
    other = lax.rem(position, 4) == 0

    for height in range(levels, 1, -1):
        offset = 2 ** (height - 1)
        mails = level_mail[height]
        if height < levels:
            pl.when(holds(height))(functools.partial(sends, height, start))

        @pl.when(lax.rem(position, 2**height) == offset)
        def _():
            mails["c_up"].wait_recv(me)
            if height == levels:
                flipped = coup[...].T
            else:
                from_below = jnp.where(coupled(height), 1.0, 0.0)
                value = coup[...].astype(jnp.float32)
                flipped = jnp.where(from_below > 0.5, value.T, value).astype(jnp.bfloat16)
            if height == 2:
                mails["b"].wait_recv(me)
                mirror(diag_b)
                odd_b.start(diag_b, near(1))
            else:
                mails["b"].wait_recv(me)
                mirror(diag_b)
            toward_upper = product_transposed(low[...], flipped) + product(upp[...], diag_b[...])
            up[...] = toward_upper.astype(jnp.bfloat16)
            if height == 2:
                coup1[...] = up[...].T
                odd_c.start(coup1, near(1))
            mails["a"].wait_recv(me)
            mirror(diag_a)
            toward_lower = product(low[...], diag_a[...]) + product(upp[...], flipped)
            down[...] = toward_lower.astype(jnp.bfloat16)
            if height == 2:
                feed_c.start(down, near(-2))
            diagonal = (
                inv[...].astype(jnp.float32)
                + product_transposed(down[...], low[...])
                + product_transposed(up[...], upp[...])
            )
            diag[...] = diagonal.astype(jnp.bfloat16)
            if height == 2:
                feed_b.start(diag, near(-2))
                diag_b1[...] = diag_b[...]

    @pl.when(even)
    def _():
        odd_a.start(diag, near(1))
        store(diag, out_diag.at[0], 0).start()
        diag_a1[...] = diag[...]
        back_low.wait_recv(me)
        back_upp.wait_recv(me)

    @pl.when(other)
    def _():
        odd_c.relay(feed_c, near(1))
        odd_b.relay(feed_b, near(1))
        mirror(diag_b1)

    @pl.when(odd)
    def _():
        load(sep_lower, low1, 0).wait()
        load(sep_upper, upp1, 1).wait()
        load(sep_inv, inv1, 2).wait()
        odd_b.wait_recv(me)
        mirror(diag_b1)
        odd_c.wait_recv(me)

    toward_upper = product_transposed(low1[...], coup1[...]) + product(upp1[...], diag_b1[...])
    up1[...] = toward_upper.astype(jnp.bfloat16)

    @pl.when(odd)
    def _():
        odd_a.wait_recv(me)
        mirror(diag_a1)

    toward_lower = product(low1[...], diag_a1[...]) + product(upp1[...], coup1[...])
    down1[...] = toward_lower.astype(jnp.bfloat16)

    @pl.when(even)
    def _():
        back_inv.wait_recv(me)
        mirror(inv1)

    diagonal = (
        inv1[...].astype(jnp.float32)
        + product_transposed(down1[...], low1[...])
        + product_transposed(up1[...], upp1[...])
    )
    diag1[...] = diagonal.astype(jnp.bfloat16)

    load(int_lower, ilow, 5).wait()
    load(int_upper, iupp, 6).wait()
    load(int_inv, iinv, 7).wait()

    def interior(own, coupling, following):
        own_value = (product(ilow[...], own[...]) + product(iupp[...], coupling)).astype(
            jnp.bfloat16
        )
        below[...] = own_value
        store(below, out_below.at[0], 1).start()
        next_value = (
            product_transposed(ilow[...], coupling) + product(iupp[...], following[...])
        ).astype(jnp.bfloat16)
        below_t[...] = next_value.T
        store(below_t, out_below.at[1], 2).start()
        diagonal = (
            iinv[...].astype(jnp.float32)
            + product_transposed(own_value, ilow[...])
            + product_transposed(next_value, iupp[...])
        )
        idiag[...] = diagonal.astype(jnp.bfloat16)
        store(idiag, out_diag.at[1], 3).start()

    @pl.when(odd)
    def _():
        store(diag1, out_diag.at[0], 0).start()
        interior(diag1, up1[...].T, diag_b1)

    @pl.when(even)
    def _():
        interior(diag_a1, down1[...], diag1)

    for height in range(levels, 1, -1):
        pl.when(holds(height))(functools.partial(sends, height, finish))

    @pl.when(parent)
    def _():
        feed_c.wait_send(down, near(-2))
        feed_b.wait_send(diag, near(-2))

    @pl.when(even)
    def _():
        odd_a.wait_send(diag, near(1))
        odd_b.wait_send(diag_b1, near(1))
        odd_c.wait_send(coup1, near(1))

    @pl.when(odd)
    def _():
        back_low.wait_send(sep_lower.at[0], near(-1))
        back_upp.wait_send(sep_upper.at[0], near(-1))
        back_inv.wait_send(sep_inv.at[0], near(-1))

    store(diag, out_diag.at[0], 0).wait()
    store(below, out_below.at[0], 1).wait()
    store(below_t, out_below.at[1], 2).wait()
    store(idiag, out_diag.at[1], 3).wait()


def solution(mesh):
    devices = mesh.shape["tm"]
    levels = min(4, devices // 4)

    def on_device(*blocks):
        size = blocks[0].shape[-1]
        sends, receives = semaphore_counts(levels, len(strips(size)))
        block = pltpu.VMEM((size, size), jnp.bfloat16)
        out = jax.ShapeDtypeStruct((2, size, size), jnp.bfloat16)
        return pl.pallas_call(
            functools.partial(kernel, devices, levels),
            out_shape=(out, out),
            in_specs=[pl.BlockSpec(memory_space=pl.ANY)] * len(blocks),
            out_specs=[pl.BlockSpec(memory_space=pl.ANY)] * 2,
            scratch_shapes=[block] * 24
            + [
                pltpu.SemaphoreType.DMA((sends,)),
                pltpu.SemaphoreType.DMA((receives,)),
                pltpu.SemaphoreType.DMA((8,)),
                pltpu.SemaphoreType.DMA((4,)),
            ],
            compiler_params=pltpu.CompilerParams(
                collective_id=0, has_side_effects=True, vmem_limit_bytes=40 * 2**20
            ),
            cost_estimate=pl.CostEstimate(
                flops=36 * size**3, bytes_accessed=24 * size**2, transcendentals=0
            ),
        )(*blocks)

    spec = P(("rep", "tm"), None, None)
    return jax.shard_map(
        on_device, mesh=mesh, in_specs=(spec,) * 8, out_specs=(spec, spec), check_vma=False
    )
```

time: 72.8 us -> 52.7 us (0.72)
  the two profiles are of different devices: /device:TPU:0 before, /device:TPU:28 now
where the time goes in v1:
time: 52.7 us; the launch traced here: 52.3 us
  Pallas kernels  42.3 us (80%)
  local copies, waits for them, and re-layouts  9.31 us (18%)
  between operations  0.66 us (1%)
    pallas_call x1, Pallas kernels, on_device(): pl.pallas_call(functools.partial(kernel, devices, levels), out_shape=(out...  42.3 us
    unnamed x18, local copies, waits for them, and re-layouts  9.31 us

profile of v1, /device:TPU:28, one launch (start us, length us, event | category | flops | bytes accessed | tf_op | source)
XLA Modules:
  0.0 52.3 jit_solution(1583500401654717537)
XLA Ops:
  0.6 0.0 copy-start
  0.6 1.0 %copy-done = bf16[1,384,384]{2,1,0:T(8,128)(2,1)S(1)} copy-done((bf16[1,384,384]{2,1,0:T(8,128)(2,1)S(1)}, bf16[1,384,384]{2,1,0:T(8,128)(2,1)}, u32[]{:S(2)}) %copy-start) | copy-done | bytes 294936
  1.6 0.0 copy-start.1
  1.6 1.0 %copy-done.1 = bf16[1,384,384]{2,1,0:T(8,128)(2,1)S(1)} copy-done((bf16[1,384,384]{2,1,0:T(8,128)(2,1)S(1)}, bf16[1,384,384]{2,1,0:T(8,128)(2,1)}, u32[]{:S(2)}) %copy-start.1) | copy-done | bytes 294936
  2.6 0.0 copy-start.2
  2.6 1.0 %copy-done.2 = bf16[1,384,384]{2,1,0:T(8,128)(2,1)S(1)} copy-done((bf16[1,384,384]{2,1,0:T(8,128)(2,1)S(1)}, bf16[1,384,384]{2,1,0:T(8,128)(2,1)}, u32[]{:S(2)}) %copy-start.2) | copy-done | bytes 294936
  3.5 0.0 copy-start.3
  3.5 1.0 %copy-done.3 = bf16[1,384,384]{2,1,0:T(8,128)(2,1)S(1)} copy-done((bf16[1,384,384]{2,1,0:T(8,128)(2,1)S(1)}, bf16[1,384,384]{2,1,0:T(8,128)(2,1)}, u32[]{:S(2)}) %copy-start.3) | copy-done | bytes 294936
  4.5 0.0 copy-start.4
  4.5 1.0 %copy-done.4 = bf16[1,384,384]{2,1,0:T(8,128)(2,1)S(1)} copy-done((bf16[1,384,384]{2,1,0:T(8,128)(2,1)S(1)}, bf16[1,384,384]{2,1,0:T(8,128)(2,1)}, u32[]{:S(2)}) %copy-start.4) | copy-done | bytes 294936
  5.4 0.0 copy-start.5
  5.4 1.0 %copy-done.5 = bf16[1,384,384]{2,1,0:T(8,128)(2,1)S(1)} copy-done((bf16[1,384,384]{2,1,0:T(8,128)(2,1)S(1)}, bf16[1,384,384]{2,1,0:T(8,128)(2,1)}, u32[]{:S(2)}) %copy-start.5) | copy-done | bytes 294936
  6.4 0.0 copy-start.6
  6.4 1.0 %copy-done.6 = bf16[1,384,384]{2,1,0:T(8,128)(2,1)S(1)} copy-done((bf16[1,384,384]{2,1,0:T(8,128)(2,1)S(1)}, bf16[1,384,384]{2,1,0:T(8,128)(2,1)}, u32[]{:S(2)}) %copy-start.6) | copy-done | bytes 294936
  7.4 0.0 copy-start.7
  7.4 1.0 %copy-done.7 = bf16[1,384,384]{2,1,0:T(8,128)(2,1)S(1)} copy-done((bf16[1,384,384]{2,1,0:T(8,128)(2,1)S(1)}, bf16[1,384,384]{2,1,0:T(8,128)(2,1)}, u32[]{:S(2)}) %copy-start.7) | copy-done | bytes 294936
  8.3 42.3 %shard_map.95 = (bf16[2,384,384]{2,1,0:T(8,128)(2,1)S(1)}, bf16[2,384,384]{2,1,0:T(8,128)(2,1)S(1)}) custom-call(bf16[1,384,384]{2,1,0:T(8,128)(2,1)S(1)} %copy-done, bf16[1,384,384]{2,1,0:T(8,128)(2,1)S(1)} %copy-done.1, bf16[1,384,384]{2,1,0:T(8,128)(2,1)S(1)} %copy-done.2, bf16[1,384,384]{2,1,0:T(8,128)(2,1)S(1)} %copy-done.3, ...), custom_call_target="tpu_custom_call" | custom-call | flops 2038431744 | bytes 3538944 | tf_op jit(solution)/shard_map/pallas_call | solution.py:417
  50.7 0.8 %copy.12 = bf16[2,384,384]{2,1,0:T(8,128)(2,1)} copy(bf16[2,384,384]{2,1,0:T(8,128)(2,1)S(1)} %get-tuple-element.4) | data formatting | bytes 1179648
  51.5 0.8 %copy.13 = bf16[2,384,384]{2,1,0:T(8,128)(2,1)} copy(bf16[2,384,384]{2,1,0:T(8,128)(2,1)S(1)} %get-tuple-element.5) | data formatting | bytes 1179648
Async XLA Ops:
  0.6 1.0 %copy-start = (bf16[1,384,384]{2,1,0:T(8,128)(2,1)S(1)}, bf16[1,384,384]{2,1,0:T(8,128)(2,1)}, u32[]{:S(2)}) copy-start(bf16[1,384,384]{2,1,0:T(8,128)(2,1)} %sep_inv.1) | copy-start | bytes 884740
  1.6 1.0 %copy-start.1 = (bf16[1,384,384]{2,1,0:T(8,128)(2,1)S(1)}, bf16[1,384,384]{2,1,0:T(8,128)(2,1)}, u32[]{:S(2)}) copy-start(bf16[1,384,384]{2,1,0:T(8,128)(2,1)} %sep_lower.1) | copy-start | bytes 884740
  2.6 1.0 %copy-start.2 = (bf16[1,384,384]{2,1,0:T(8,128)(2,1)S(1)}, bf16[1,384,384]{2,1,0:T(8,128)(2,1)}, u32[]{:S(2)}) copy-start(bf16[1,384,384]{2,1,0:T(8,128)(2,1)} %sep_upper.1) | copy-start | bytes 884740
  3.5 1.0 %copy-start.3 = (bf16[1,384,384]{2,1,0:T(8,128)(2,1)S(1)}, bf16[1,384,384]{2,1,0:T(8,128)(2,1)}, u32[]{:S(2)}) copy-start(bf16[1,384,384]{2,1,0:T(8,128)(2,1)} %top_diag.1) | copy-start | bytes 884740
  4.5 1.0 %copy-start.4 = (bf16[1,384,384]{2,1,0:T(8,128)(2,1)S(1)}, bf16[1,384,384]{2,1,0:T(8,128)(2,1)}, u32[]{:S(2)}) copy-start(bf16[1,384,384]{2,1,0:T(8,128)(2,1)} %top_coup.1) | copy-start | bytes 884740
  5.4 1.0 %copy-start.5 = (bf16[1,384,384]{2,1,0:T(8,128)(2,1)S(1)}, bf16[1,384,384]{2,1,0:T(8,128)(2,1)}, u32[]{:S(2)}) copy-start(bf16[1,384,384]{2,1,0:T(8,128)(2,1)} %int_inv.1) | copy-start | bytes 884740
  6.4 1.0 %copy-start.6 = (bf16[1,384,384]{2,1,0:T(8,128)(2,1)S(1)}, bf16[1,384,384]{2,1,0:T(8,128)(2,1)}, u32[]{:S(2)}) copy-start(bf16[1,384,384]{2,1,0:T(8,128)(2,1)} %int_lower.1) | copy-start | bytes 884740
  7.4 1.0 %copy-start.7 = (bf16[1,384,384]{2,1,0:T(8,128)(2,1)S(1)}, bf16[1,384,384]{2,1,0:T(8,128)(2,1)}, u32[]{:S(2)}) copy-start(bf16[1,384,384]{2,1,0:T(8,128)(2,1)} %int_upper.1) | copy-start | bytes 884740

commit v2 on v1

--- a/solution.py
+++ b/solution.py
@@ -26,9 +26,10 @@
     return [(at, tile) for at in range(0, size, tile)]
 
 
-def strip(ref, at, rows):
+def strip(ref, at, rows, symmetric):
     size = ref.shape[-1]
-    return ref.at[pl.ds(at, rows), pl.ds(at, size - at)]
+    first = at if symmetric else 0
+    return ref.at[pl.ds(at, rows), pl.ds(first, size - first)]
 
 
 def mirror(ref):
@@ -45,15 +46,13 @@
         self.dst, self.symmetric = dst, symmetric
         self.send_sem, self.send_at = send_sem, send_at
         self.recv_sem, self.recv_at = recv_sem, recv_at
-        self.pieces = strips(dst.shape[-1]) if symmetric else [None]
+        self.pieces = strips(dst.shape[-1])
 
     def copy(self, src, to, piece):
-        dst = self.dst
-        if self.symmetric:
-            src, dst = strip(src, *self.pieces[piece]), strip(dst, *self.pieces[piece])
+        part = (*self.pieces[piece], self.symmetric)
         return pltpu.make_async_remote_copy(
-            src_ref=src,
-            dst_ref=dst,
+            src_ref=strip(src, *part),
+            dst_ref=strip(self.dst, *part),
             send_sem=self.send_sem.at[self.send_at + piece],
             recv_sem=self.recv_sem.at[self.recv_at + piece],
             device_id={"tm": to},
@@ -79,10 +78,7 @@
 
 
 def semaphore_counts(levels, pieces):
-    per_level = 2 * pieces + 2
-    sends = (levels - 1) * per_level + (1 + pieces) + (1 + 2 * pieces) + (2 + pieces)
-    receives = (1 + 2 * pieces) + (3 + 3 * pieces)
-    return sends, receives
+    return (4 * (levels - 1) + 10) * pieces, 9 * pieces
 
 
 def kernel(
@@ -152,10 +148,10 @@
         return counts[kind] - number
 
     def receives(symmetric):
-        return take("recv", pieces if symmetric else 1)
+        return take("recv", pieces)
 
     def mail(dst, recv_at, symmetric):
-        send_at = take("send", pieces if symmetric else 1)
+        send_at = take("send", pieces)
         return Mail(dst, send_sem, send_at, recv_sem, recv_at, symmetric)
 
     at_a, at_b, at_c = receives(True), receives(True), receives(False)
@@ -170,7 +166,12 @@
             c_down=mail(coup, at_c, False),
         )
     feed_c, feed_b = mail(coup1, at_c1, False), mail(diag_b1, at_b1, True)
-    odd_a, odd_b, odd_c = mail(diag_a1, at_a1, True), mail(diag_b1, at_b1, True), mail(coup1, at_c1, False)
+    odd_a, odd_b, odd_c = (
+        mail(diag_a1, at_a1, True),
+        mail(diag_b1, at_b1, True),
+        mail(coup1, at_c1, False),
+    )
+    rail_b, even_b = mail(diag_b1, at_b1, True), mail(diag_b1, at_b1, True)
     back_inv, back_low, back_upp = (
         mail(inv1, at_inv1, True),
         mail(low1, at_low1, False),
@@ -228,8 +229,9 @@
         else:
             pl.when(coupled(height))(act_up)
             pl.when(coupled(height))(act_down)
-        act(mails["b"], diag_src, near(-offset))
         act(mails["a"], diag_src, near(offset))
+        if height > 2:
+            act(mails["b"], diag_src, near(-offset))
 
     def start(message, src, to):
         message.start(src, to)
@@ -237,13 +239,33 @@
     def finish(message, src, to):
         message.wait_send(src, to)
 
-    pl.when(holds(levels))(lambda: sends(levels, start))
+    parent = lax.rem(position, 4) == 2
+    other = lax.rem(position, 4) == 0
+    first_odd = lax.rem(position, 4) == 1
+    last_odd = lax.rem(position, 4) == 3
+
+    @pl.when(top)
+    def _():
+        odd_a.start(top_diag.at[0], near(1))
+        sends(levels, start)
 
     @pl.when(odd)
     def _():
         back_low.start(sep_lower.at[0], near(-1))
+
+    @pl.when(first_odd)
+    def _():
         back_upp.start(sep_upper.at[0], near(-1))
         back_inv.start(sep_inv.at[0], near(-1))
+        rail_b.relay(odd_a, near(-2))
+        mirror(diag_a1)
+
+    @pl.when(last_odd)
+    def _():
+        even_b.relay(rail_b, near(-1))
+        back_upp.start(sep_upper.at[0], near(-1))
+        back_inv.start(sep_inv.at[0], near(-1))
+        mirror(diag_b1)
 
     @pl.when(even)
     def _():
@@ -254,9 +276,6 @@
     @pl.when(top)
     def _():
         load(top_diag, diag, 3).wait()
-
-    parent = lax.rem(position, 4) == 2
-    other = lax.rem(position, 4) == 0
 
     for height in range(levels, 1, -1):
         offset = 2 ** (height - 1)
@@ -274,13 +293,13 @@
                 value = coup[...].astype(jnp.float32)
                 flipped = jnp.where(from_below > 0.5, value.T, value).astype(jnp.bfloat16)
             if height == 2:
-                mails["b"].wait_recv(me)
-                mirror(diag_b)
-                odd_b.start(diag_b, near(1))
+                even_b.wait_recv(me)
+                upper = diag_b1
             else:
                 mails["b"].wait_recv(me)
-                mirror(diag_b)
-            toward_upper = product_transposed(low[...], flipped) + product(upp[...], diag_b[...])
+                upper = diag_b
+            mirror(upper)
+            toward_upper = product_transposed(low[...], flipped) + product(upp[...], upper[...])
             up[...] = toward_upper.astype(jnp.bfloat16)
             if height == 2:
                 coup1[...] = up[...].T
@@ -297,13 +316,12 @@
                 + product_transposed(up[...], upp[...])
             )
             diag[...] = diagonal.astype(jnp.bfloat16)
+            odd_a.start(diag, near(1))
             if height == 2:
                 feed_b.start(diag, near(-2))
-                diag_b1[...] = diag_b[...]
-
-    @pl.when(even)
-    def _():
-        odd_a.start(diag, near(1))
+
+    @pl.when(even)
+    def _():
         store(diag, out_diag.at[0], 0).start()
         diag_a1[...] = diag[...]
         back_low.wait_recv(me)
@@ -320,14 +338,17 @@
         load(sep_lower, low1, 0).wait()
         load(sep_upper, upp1, 1).wait()
         load(sep_inv, inv1, 2).wait()
+        odd_c.wait_recv(me)
+
+    @pl.when(first_odd)
+    def _():
         odd_b.wait_recv(me)
         mirror(diag_b1)
-        odd_c.wait_recv(me)
 
     toward_upper = product_transposed(low1[...], coup1[...]) + product(upp1[...], diag_b1[...])
     up1[...] = toward_upper.astype(jnp.bfloat16)
 
-    @pl.when(odd)
+    @pl.when(last_odd)
     def _():
         odd_a.wait_recv(me)
         mirror(diag_a1)
@@ -390,8 +411,19 @@
     @pl.when(even)
     def _():
         odd_a.wait_send(diag, near(1))
+        odd_c.wait_send(coup1, near(1))
+
+    @pl.when(other)
+    def _():
         odd_b.wait_send(diag_b1, near(1))
-        odd_c.wait_send(coup1, near(1))
+
+    @pl.when(first_odd)
+    def _():
+        rail_b.wait_send(diag_a1, near(-2))
+
+    @pl.when(last_odd)
+    def _():
+        even_b.wait_send(diag_b1, near(-1))
 
     @pl.when(odd)
     def _():
@@ -417,8 +449,8 @@
         return pl.pallas_call(
             functools.partial(kernel, devices, levels),
             out_shape=(out, out),
-            in_specs=[pl.BlockSpec(memory_space=pl.ANY)] * len(blocks),
-            out_specs=[pl.BlockSpec(memory_space=pl.ANY)] * 2,
+            in_specs=[pl.BlockSpec(memory_space=pltpu.HBM)] * len(blocks),
+            out_specs=[pl.BlockSpec(memory_space=pltpu.HBM)] * 2,
             scratch_shapes=[block] * 24
             + [
                 pltpu.SemaphoreType.DMA((sends,)),
@@ -427,7 +459,7 @@
                 pltpu.SemaphoreType.DMA((4,)),
             ],
             compiler_params=pltpu.CompilerParams(
-                collective_id=0, has_side_effects=True, vmem_limit_bytes=40 * 2**20
+                collective_id=0, has_side_effects=True, vmem_limit_bytes=63 * 2**20
             ),
             cost_estimate=pl.CostEstimate(
                 flops=36 * size**3, bytes_accessed=24 * size**2, transcendentals=0

time: 52.7 us -> 40.2 us (0.76)
  local copies, waits for them, and re-layouts: 9.31 us -> 2.82 us
  Pallas kernels: 42.3 us -> 36.5 us
    unnamed x18 -> x4, local copies, waits for them, and re-layouts: 9.31 us -> 2.82 us
    pallas_call x1, Pallas kernels: 42.3 us -> 36.5 us  [on_device(): pl.pallas_call(functools.partial(kernel, devices, levels), out_shape=(out...]
where the time goes in v2:
time: 40.2 us; the launch traced here: 40 us
  Pallas kernels  36.5 us (91%)
  local copies, waits for them, and re-layouts  2.82 us (7%)
  between operations  0.65 us (2%)
    pallas_call x1, Pallas kernels, on_device(): pl.pallas_call(functools.partial(kernel, devices, levels), out_shape=(out...  36.5 us
    unnamed x4, local copies, waits for them, and re-layouts  2.82 us

profile of v2, /device:TPU:28, one launch (start us, length us, event | category | flops | bytes accessed | tf_op | source)
XLA Modules:
  0.0 40.0 jit_solution(1365743169541615471)
XLA Ops:
  0.6 36.5 %shard_map.95 = (bf16[2,384,384]{2,1,0:T(8,128)(2,1)}, bf16[2,384,384]{2,1,0:T(8,128)(2,1)}) custom-call(bf16[1,384,384]{2,1,0:T(8,128)(2,1)} %sep_inv.1, bf16[1,384,384]{2,1,0:T(8,128)(2,1)} %sep_lower.1, bf16[1,384,384]{2,1,0:T(8,128)(2,1)} %sep_upper.1, bf16[1,384,384]{2,1,0:T(8,128)(2,1)} %top_diag.1, bf16[1,384,384]{2,1,0:T(8,128)(2,1)} %top_coup.1, ...), custom_call_target="tpu_custom_call" | custom-call | flops 2038431744 | bytes 3538944 | tf_op jit(solution)/shard_map/pallas_call | solution.py:449
  37.2 0.0 copy-start
  37.2 2.0 %copy.12 = bf16[2,384,384]{2,1,0:T(8,128)(2,1)} copy(bf16[2,384,384]{2,1,0:T(8,128)(2,1)} %get-tuple-element.4) | data formatting | bytes 1179648
  39.2 0.0 copy-done
  39.2 0.8 %copy.13 = bf16[2,384,384]{2,1,0:T(8,128)(2,1)} copy(bf16[2,384,384]{2,1,0:T(8,128)(2,1)S(1)} %copy-done) | data formatting | bytes 1179648
Async XLA Ops:
  37.2 2.0 %copy-start = (bf16[2,384,384]{2,1,0:T(8,128)(2,1)S(1)}, bf16[2,384,384]{2,1,0:T(8,128)(2,1)}, u32[]{:S(2)}) copy-start(bf16[2,384,384]{2,1,0:T(8,128)(2,1)} %get-tuple-element.5) | copy-start | bytes 1769476

commit v3 on v2

--- a/solution.py
+++ b/solution.py
@@ -115,13 +115,12 @@
     iinv,
     ilow,
     iupp,
-    idiag,
-    below,
-    below_t,
+    part_side,
+    part_diag,
+    part_int,
     send_sem,
     recv_sem,
     load_sem,
-    store_sem,
 ):
     size = sep_inv.shape[-1]
     pieces = len(strips(size))
@@ -137,9 +136,6 @@
 
     def load(src, dst, at):
         return pltpu.make_async_copy(src.at[0], dst, load_sem.at[at])
-
-    def store(src, dst, at):
-        return pltpu.make_async_copy(src, dst, store_sem.at[at])
 
     counts = {"send": 0, "recv": 0}
 
@@ -292,24 +288,28 @@
                 from_below = jnp.where(coupled(height), 1.0, 0.0)
                 value = coup[...].astype(jnp.float32)
                 flipped = jnp.where(from_below > 0.5, value.T, value).astype(jnp.bfloat16)
-            if height == 2:
-                even_b.wait_recv(me)
-                upper = diag_b1
-            else:
-                mails["b"].wait_recv(me)
-                upper = diag_b
-            mirror(upper)
-            toward_upper = product_transposed(low[...], flipped) + product(upp[...], upper[...])
-            up[...] = toward_upper.astype(jnp.bfloat16)
-            if height == 2:
-                coup1[...] = up[...].T
-                odd_c.start(coup1, near(1))
+            def upper_side():
+                if height == 2:
+                    even_b.wait_recv(me)
+                else:
+                    mails["b"].wait_recv(me)
+                upper = diag_b1 if height == 2 else diag_b
+                mirror(upper)
+                toward_upper = product_transposed(low[...], flipped) + product(
+                    upp[...], upper[...]
+                )
+                up[...] = toward_upper.astype(jnp.bfloat16)
+                if height == 2:
+                    coup1[...] = up[...].T
+                    odd_c.start(coup1, near(1))
+
             mails["a"].wait_recv(me)
             mirror(diag_a)
             toward_lower = product(low[...], diag_a[...]) + product(upp[...], flipped)
             down[...] = toward_lower.astype(jnp.bfloat16)
             if height == 2:
                 feed_c.start(down, near(-2))
+            upper_side()
             diagonal = (
                 inv[...].astype(jnp.float32)
                 + product_transposed(down[...], low[...])
@@ -320,85 +320,121 @@
             if height == 2:
                 feed_b.start(diag, near(-2))
 
+    late_b = lax.rem(position, 4) < 2
+    late_a = lax.rem(position, 4) >= 2
+
+    load(int_lower, ilow, 5).wait()
+    load(int_upper, iupp, 6).wait()
+    load(int_inv, iinv, 7).wait()
+
+    def interior_own(own, coupling):
+        value = (product(ilow[...], own[...]) + product(iupp[...], coupling)).astype(jnp.bfloat16)
+        out_below[0] = value
+        return product_transposed(value, ilow[...])
+
+    def interior_next(coupling_product, following):
+        value = (coupling_product + product(iupp[...], following[...])).astype(jnp.bfloat16)
+        out_below[1] = value.T
+        return product_transposed(value, iupp[...])
+
+    def finish_interior(value):
+        out_diag[1] = (part_int[...] + value).astype(jnp.bfloat16)
+
     @pl.when(even)
     def _():
-        store(diag, out_diag.at[0], 0).start()
+        out_diag[0] = diag[...]
         diag_a1[...] = diag[...]
-        back_low.wait_recv(me)
-        back_upp.wait_recv(me)
-
-    @pl.when(other)
-    def _():
-        odd_c.relay(feed_c, near(1))
-        odd_b.relay(feed_b, near(1))
-        mirror(diag_b1)
 
     @pl.when(odd)
     def _():
         load(sep_lower, low1, 0).wait()
         load(sep_upper, upp1, 1).wait()
         load(sep_inv, inv1, 2).wait()
-        odd_c.wait_recv(me)
-
-    @pl.when(first_odd)
-    def _():
-        odd_b.wait_recv(me)
-        mirror(diag_b1)
-
-    toward_upper = product_transposed(low1[...], coup1[...]) + product(upp1[...], diag_b1[...])
-    up1[...] = toward_upper.astype(jnp.bfloat16)
-
-    @pl.when(last_odd)
-    def _():
-        odd_a.wait_recv(me)
-        mirror(diag_a1)
-
-    toward_lower = product(low1[...], diag_a1[...]) + product(upp1[...], coup1[...])
-    down1[...] = toward_lower.astype(jnp.bfloat16)
-
-    @pl.when(even)
-    def _():
+
+    @pl.when(other)
+    def _():
+        odd_c.relay(feed_c, near(1))
+        back_low.wait_recv(me)
+        back_upp.wait_recv(me)
         back_inv.wait_recv(me)
         mirror(inv1)
 
-    diagonal = (
-        inv1[...].astype(jnp.float32)
-        + product_transposed(down1[...], low1[...])
-        + product_transposed(up1[...], upp1[...])
-    )
-    diag1[...] = diagonal.astype(jnp.bfloat16)
-
-    load(int_lower, ilow, 5).wait()
-    load(int_upper, iupp, 6).wait()
-    load(int_inv, iinv, 7).wait()
-
-    def interior(own, coupling, following):
-        own_value = (product(ilow[...], own[...]) + product(iupp[...], coupling)).astype(
-            jnp.bfloat16
-        )
-        below[...] = own_value
-        store(below, out_below.at[0], 1).start()
-        next_value = (
-            product_transposed(ilow[...], coupling) + product(iupp[...], following[...])
-        ).astype(jnp.bfloat16)
-        below_t[...] = next_value.T
-        store(below_t, out_below.at[1], 2).start()
-        diagonal = (
-            iinv[...].astype(jnp.float32)
-            + product_transposed(own_value, ilow[...])
-            + product_transposed(next_value, iupp[...])
-        )
-        idiag[...] = diagonal.astype(jnp.bfloat16)
-        store(idiag, out_diag.at[1], 3).start()
-
     @pl.when(odd)
     def _():
-        store(diag1, out_diag.at[0], 0).start()
-        interior(diag1, up1[...].T, diag_b1)
-
-    @pl.when(even)
-    def _():
-        interior(diag_a1, down1[...], diag1)
+        odd_c.wait_recv(me)
+
+    @pl.when(late_b)
+    def _():
+        toward_lower = product(low1[...], diag_a1[...]) + product(upp1[...], coup1[...])
+        down1[...] = toward_lower.astype(jnp.bfloat16)
+        part_side[...] = product_transposed(low1[...], coup1[...])
+        part_diag[...] = inv1[...].astype(jnp.float32) + product_transposed(down1[...], low1[...])
+
+        @pl.when(even)
+        def _():
+            part_int[...] = iinv[...].astype(jnp.float32) + interior_own(diag_a1, down1[...])
+            odd_b.relay(feed_b, near(1))
+
+        @pl.when(odd)
+        def _():
+            odd_b.wait_recv(me)
+
+        mirror(diag_b1)
+        up1[...] = (part_side[...] + product(upp1[...], diag_b1[...])).astype(jnp.bfloat16)
+        diagonal = part_diag[...] + product_transposed(up1[...], upp1[...])
+        diag1[...] = diagonal.astype(jnp.bfloat16)
+
+        @pl.when(even)
+        def _():
+            finish_interior(interior_next(product_transposed(ilow[...], down1[...]), diag1))
+
+        @pl.when(odd)
+        def _():
+            out_diag[0] = diag1[...]
+            part_int[...] = iinv[...].astype(jnp.float32) + interior_next(
+                product(ilow[...], up1[...]), diag_b1
+            )
+            finish_interior(interior_own(diag1, up1[...].T))
+
+    @pl.when(late_a)
+    def _():
+        @pl.when(even)
+        def _():
+            back_low.wait_recv(me)
+            back_upp.wait_recv(me)
+
+        toward_upper = product_transposed(low1[...], coup1[...]) + product(upp1[...], diag_b1[...])
+        up1[...] = toward_upper.astype(jnp.bfloat16)
+        part_side[...] = product(upp1[...], coup1[...])
+        part_diag[...] = product_transposed(up1[...], upp1[...])
+
+        @pl.when(odd)
+        def _():
+            part_diag[...] += inv1[...].astype(jnp.float32)
+            part_int[...] = iinv[...].astype(jnp.float32) + interior_next(
+                product(ilow[...], up1[...]), diag_b1
+            )
+            odd_a.wait_recv(me)
+            mirror(diag_a1)
+
+        toward_lower = product(low1[...], diag_a1[...]) + part_side[...]
+        down1[...] = toward_lower.astype(jnp.bfloat16)
+        part_diag[...] += product_transposed(down1[...], low1[...])
+
+        @pl.when(even)
+        def _():
+            part_int[...] = iinv[...].astype(jnp.float32) + interior_own(diag_a1, down1[...])
+            part_side[...] = product_transposed(ilow[...], down1[...])
+            back_inv.wait_recv(me)
+            mirror(inv1)
+            diag1[...] = (part_diag[...] + inv1[...].astype(jnp.float32)).astype(jnp.bfloat16)
+            finish_interior(interior_next(part_side[...], diag1))
+
+        @pl.when(odd)
+        def _():
+            diag1[...] = part_diag[...].astype(jnp.bfloat16)
+            out_diag[0] = diag1[...]
+            finish_interior(interior_own(diag1, up1[...].T))
 
     for height in range(levels, 1, -1):
         pl.when(holds(height))(functools.partial(sends, height, finish))
@@ -431,10 +467,26 @@
         back_upp.wait_send(sep_upper.at[0], near(-1))
         back_inv.wait_send(sep_inv.at[0], near(-1))
 
-    store(diag, out_diag.at[0], 0).wait()
-    store(below, out_below.at[0], 1).wait()
-    store(below_t, out_below.at[1], 2).wait()
-    store(idiag, out_diag.at[1], 3).wait()
+
+def hand_over(diag_from, below_from, diag_to, below_to, held, in_sem, out_sem):
+    pairs = [
+        (src.at[at], dst.at[at])
+        for src, dst in ((diag_from, diag_to), (below_from, below_to))
+        for at in range(2)
+    ]
+    ins = [
+        pltpu.make_async_copy(src, held.at[at], in_sem.at[at]) for at, (src, _) in enumerate(pairs)
+    ]
+    outs = [
+        pltpu.make_async_copy(held.at[at], dst, out_sem.at[at]) for at, (_, dst) in enumerate(pairs)
+    ]
+    for copy in ins:
+        copy.start()
+    for into, out in zip(ins, outs):
+        into.wait()
+        out.start()
+    for copy in outs:
+        copy.wait()
 
 
 def solution(mesh):
@@ -446,17 +498,17 @@
         sends, receives = semaphore_counts(levels, len(strips(size)))
         block = pltpu.VMEM((size, size), jnp.bfloat16)
         out = jax.ShapeDtypeStruct((2, size, size), jnp.bfloat16)
-        return pl.pallas_call(
+        found = pl.pallas_call(
             functools.partial(kernel, devices, levels),
             out_shape=(out, out),
             in_specs=[pl.BlockSpec(memory_space=pltpu.HBM)] * len(blocks),
-            out_specs=[pl.BlockSpec(memory_space=pltpu.HBM)] * 2,
-            scratch_shapes=[block] * 24
+            out_specs=[pl.BlockSpec(memory_space=pltpu.VMEM)] * 2,
+            scratch_shapes=[block] * 21
+            + [pltpu.VMEM((size, size), jnp.float32)] * 3
             + [
                 pltpu.SemaphoreType.DMA((sends,)),
                 pltpu.SemaphoreType.DMA((receives,)),
                 pltpu.SemaphoreType.DMA((8,)),
-                pltpu.SemaphoreType.DMA((4,)),
             ],
             compiler_params=pltpu.CompilerParams(
                 collective_id=0, has_side_effects=True, vmem_limit_bytes=63 * 2**20
@@ -465,6 +517,20 @@
                 flops=36 * size**3, bytes_accessed=24 * size**2, transcendentals=0
             ),
         )(*blocks)
+        return pl.pallas_call(
+            hand_over,
+            out_shape=(out, out),
+            in_specs=[pl.BlockSpec(memory_space=pl.ANY)] * 2,
+            out_specs=[pl.BlockSpec(memory_space=pl.ANY)] * 2,
+            scratch_shapes=[
+                pltpu.VMEM((4, size, size), jnp.bfloat16),
+                pltpu.SemaphoreType.DMA((4,)),
+                pltpu.SemaphoreType.DMA((4,)),
+            ],
+            cost_estimate=pl.CostEstimate(
+                flops=0, bytes_accessed=16 * size**2, transcendentals=0
+            ),
+        )(*found)
 
     spec = P(("rep", "tm"), None, None)
     return jax.shard_map(

time: 40.2 us -> 38 us (0.945)
  local copies, waits for them, and re-layouts: 2.82 us -> 0 us
  Pallas kernels: 36.5 us -> 37.3 us
    unnamed x4 -> x0, local copies, waits for them, and re-layouts: 2.82 us -> none
    pallas_call x0 -> x1, Pallas kernels: none -> 2.04 us  [on_device(): pl.pallas_call(hand_over, out_shape=(out, out), in_specs=[pl.BlockSpec(me...]
    pallas_call x1, Pallas kernels: 36.5 us -> 35.2 us  [on_device(): pl.pallas_call(functools.partial(kernel, devices, levels), out_shape=(out...]
where the time goes in v3:
time: 38 us; the launch traced here: 37.9 us
  Pallas kernels  37.3 us (98%)
  between operations  0.64 us (2%)
    pallas_call x1, Pallas kernels, on_device(): pl.pallas_call(functools.partial(kernel, devices, levels), out_shape=(out...  35.2 us
    pallas_call x1, Pallas kernels, on_device(): pl.pallas_call(hand_over, out_shape=(out, out), in_specs=[pl.BlockSpec(me...  2.04 us

profile of v3, /device:TPU:28, one launch (start us, length us, event | category | flops | bytes accessed | tf_op | source)
XLA Modules:
  0.0 37.9 jit_solution(10166522582292783973)
XLA Ops:
  0.6 35.2 %shard_map.95 = (bf16[2,384,384]{2,1,0:T(8,128)(2,1)}, bf16[2,384,384]{2,1,0:T(8,128)(2,1)}) custom-call(bf16[1,384,384]{2,1,0:T(8,128)(2,1)} %sep_inv.1, bf16[1,384,384]{2,1,0:T(8,128)(2,1)} %sep_lower.1, bf16[1,384,384]{2,1,0:T(8,128)(2,1)} %sep_upper.1, bf16[1,384,384]{2,1,0:T(8,128)(2,1)} %top_diag.1, bf16[1,384,384]{2,1,0:T(8,128)(2,1)} %top_coup.1, ...), custom_call_target="tpu_custom_call" | custom-call | flops 2038431744 | bytes 3538944 | tf_op jit(solution)/shard_map/pallas_call | solution.py:501
  35.9 2.0 %shard_map.96 = (bf16[2,384,384]{2,1,0:T(8,128)(2,1)}, bf16[2,384,384]{2,1,0:T(8,128)(2,1)}) custom-call(bf16[2,384,384]{2,1,0:T(8,128)(2,1)} %get-tuple-element.4.diag_from, bf16[2,384,384]{2,1,0:T(8,128)(2,1)} %get-tuple-element.5.below_from), custom_call_target="tpu_custom_call" | custom-call | bytes 2359296 | tf_op jit(solution)/shard_map/pallas_call | solution.py:520
